TPU v7x, 512 devices: a whole 4x4x16 slice. The times are simulated.
512 devices in a mesh: dp: 16 (over y, x_hi, core), ctx: 32 (over z, x_lo).
Axes of the slice: x: 4 (x_hi: 2, x_lo: 2; x = x_hi * 2 + x_lo), y: 4, z: 16, core: 2. Of those that a mesh axis runs over, the one named last changes fastest.
Arguments:
- out_gate: bfloat16 [16, 8192, 512], P('dp', 'ctx'), may hold values from -6 to 6
- key_gate: bfloat16 [16, 8192, 512], P('dp', 'ctx'), may hold values from -6 to 6
- value_input: bfloat16 [16, 8192, 512], P('dp', 'ctx'), may hold values from -6 to 6
- filter_taps: bfloat16 [8192, 512], P('ctx'), may hold values from -2 to 2
- cotangent: bfloat16 [16, 8192, 512], P('dp', 'ctx'), may hold values from -6 to 6
- block_live: int32 [16, 128], P('dp', 'ctx'), may hold values 0 or 1
Outputs:
- grad_out_gate: bfloat16 [16, 8192, 512], P('dp', 'ctx')
- grad_key_gate: bfloat16 [16, 8192, 512], P('dp', 'ctx')
- grad_value: bfloat16 [16, 8192, 512], P('dp', 'ctx')
- grad_taps: bfloat16 [8192, 512], P('ctx')
Inputs may be any that keep to these rules, and one draw needn't show every extreme that they name: `block_live`: 1 where a block of 64 tokens holds sequence data, 0 where it is padding.
All inputs are finite; a program needn't handle non-finite values.
Results may differ from a plain program's by a relative error of at most 0.027.
Values may be sent and summed in bfloat16 or wider, within the bound.
A program may use at most 64 MiB of HBM per device.

v0:
```python
import math
import jax
import jax.numpy as jnp
from jax import lax
from jax.sharding import PartitionSpec as P

QLEN = 64
PROWS = 4
TWO_PI = 2.0 * math.pi


def angle_table(row_count, col_count, row_start, col_start, period_len, direction):
    row_ids = jnp.arange(row_count, dtype=jnp.int32)[:, None] + row_start
    col_ids = jnp.arange(col_count, dtype=jnp.int32)[None, :] + col_start
    phases = (row_ids * col_ids % period_len).astype(jnp.float32)
    return direction * TWO_PI * phases / period_len


def factor_tables(angles):
    return (jnp.cos(angles).astype(jnp.bfloat16), jnp.sin(angles).astype(jnp.bfloat16))


def rotate_pair(real_part, imag_part, angles):
    turn_cos = jnp.cos(angles)[None, :, :, None]
    turn_sin = jnp.sin(angles)[None, :, :, None]
    return (
        real_part * turn_cos - imag_part * turn_sin,
        real_part * turn_sin + imag_part * turn_cos,
    )


def forward_transform(signals):
    ctx_count = lax.axis_size("ctx")
    ctx_place = lax.axis_index("ctx")
    full_rows = 2 * signals.shape[1] * ctx_count
    col_count = signals.shape[2]
    col_share = col_count // ctx_count
    total_len = full_rows * col_count
    cos_rows, sin_rows = factor_tables(
        angle_table(full_rows, full_rows // 2, 0, 0, full_rows, -1.0)
    )
    twist_angles = angle_table(full_rows, col_share, 0, ctx_place * col_share, total_len, -1.0)
    cos_cols, sin_cols = factor_tables(angle_table(col_count, col_count, 0, 0, col_count, -1.0))
    spread = lax.all_to_all(signals, "ctx", split_axis=2, concat_axis=1, tiled=True)
    real_part = jnp.einsum("kp,spac->skac", cos_rows, spread, preferred_element_type=jnp.float32)
    imag_part = jnp.einsum("kp,spac->skac", sin_rows, spread, preferred_element_type=jnp.float32)
    real_part, imag_part = rotate_pair(real_part, imag_part, twist_angles)
    packed = jnp.stack([real_part, imag_part]).astype(jnp.bfloat16)
    regrouped = lax.all_to_all(packed, "ctx", split_axis=2, concat_axis=3, tiled=True)
    real_in = regrouped[0]
    imag_in = regrouped[1]
    real_out = jnp.einsum(
        "saqc,qk->sakc", real_in, cos_cols, preferred_element_type=jnp.float32
    ) - jnp.einsum("saqc,qk->sakc", imag_in, sin_cols, preferred_element_type=jnp.float32)
    imag_out = jnp.einsum(
        "saqc,qk->sakc", real_in, sin_cols, preferred_element_type=jnp.float32
    ) + jnp.einsum("saqc,qk->sakc", imag_in, cos_cols, preferred_element_type=jnp.float32)
    return jnp.stack([real_out, imag_out]).astype(jnp.bfloat16)


def inverse_transform(spectra):
    ctx_count = lax.axis_size("ctx")
    ctx_place = lax.axis_index("ctx")
    row_share = spectra.shape[2]
    col_count = spectra.shape[3]
    full_rows = row_share * ctx_count
    total_len = full_rows * col_count
    cos_cols, sin_cols = factor_tables(angle_table(col_count, col_count, 0, 0, col_count, 1.0))
    twist_angles = angle_table(row_share, col_count, ctx_place * row_share, 0, total_len, 1.0)
    cos_back, sin_back = factor_tables(angle_table(full_rows // 2, full_rows, 0, 0, full_rows, 1.0))
    real_in = spectra[0]
    imag_in = spectra[1]
    real_part = jnp.einsum(
        "sakc,kq->saqc", real_in, cos_cols, preferred_element_type=jnp.float32
    ) - jnp.einsum("sakc,kq->saqc", imag_in, sin_cols, preferred_element_type=jnp.float32)
    imag_part = jnp.einsum(
        "sakc,kq->saqc", real_in, sin_cols, preferred_element_type=jnp.float32
    ) + jnp.einsum("sakc,kq->saqc", imag_in, cos_cols, preferred_element_type=jnp.float32)
    real_part, imag_part = rotate_pair(real_part, imag_part, twist_angles)
    twisted = jnp.stack([real_part, imag_part]).astype(jnp.bfloat16)
    gathered = lax.all_to_all(twisted, "ctx", split_axis=3, concat_axis=2, tiled=True)
    signal = jnp.einsum(
        "pk,skac->spac", cos_back, gathered[0], preferred_element_type=jnp.float32
    ) - jnp.einsum("pk,skac->spac", sin_back, gathered[1], preferred_element_type=jnp.float32)
    spread = (signal * (1.0 / total_len)).astype(jnp.bfloat16)
    return lax.all_to_all(spread, "ctx", split_axis=1, concat_axis=2, tiled=True)


def spectrum_product(left_spec, right_spec, conjugate):
    left_real = left_spec[0].astype(jnp.float32)
    left_imag = left_spec[1].astype(jnp.float32)
    right_real = right_spec[0].astype(jnp.float32)
    right_imag = right_spec[1].astype(jnp.float32)
    if conjugate:
        real_out = left_real * right_real + left_imag * right_imag
        imag_out = left_imag * right_real - left_real * right_imag
    else:
        real_out = left_real * right_real - left_imag * right_imag
        imag_out = left_real * right_imag + left_imag * right_real
    return jnp.stack([real_out, imag_out]).astype(jnp.bfloat16)


def local(out_gate, key_gate, value_input, filter_taps, cotangent, block_live):
    tok_count = key_gate.shape[1]
    chan_count = key_gate.shape[2]
    block_count = block_live.shape[1]
    grid_shape = (PROWS, QLEN, chan_count)
    live_rows = block_live[0].astype(jnp.float32)[:, None, None]

    def masked(values):
        return (
            values.reshape(block_count, tok_count // block_count, chan_count) * live_rows
        ).reshape(tok_count, chan_count)

    key_wide = key_gate[0].astype(jnp.float32)
    value_wide = value_input[0].astype(jnp.float32)
    cot_wide = cotangent[0].astype(jnp.float32)
    gated_input = masked(key_wide * value_wide).astype(jnp.bfloat16).reshape(grid_shape)
    back_signal = (
        (cot_wide * out_gate[0].astype(jnp.float32)).astype(jnp.bfloat16).reshape(grid_shape)
    )
    taps_grid = filter_taps.reshape(grid_shape)
    filter_spec = None
    extra_signals = [taps_grid]
    first_spectra = forward_transform(jnp.stack([gated_input] + extra_signals))
    filter_spec = first_spectra[:, 1]
    forward_spec = first_spectra[:, 0]
    conv_out = inverse_transform(spectrum_product(forward_spec, filter_spec, False)[:, None])[0]
    backward_spec = forward_transform(back_signal[None])[:, 0]
    restored = inverse_transform(
        jnp.stack(
            [
                spectrum_product(backward_spec, filter_spec, True),
                spectrum_product(backward_spec, forward_spec, True),
            ],
            axis=1,
        )
    )
    grad_conv = restored[0]
    taps_seq = restored[1]
    conv_flat = conv_out.reshape(tok_count, chan_count).astype(jnp.float32)
    grad_gate = (cot_wide * conv_flat).astype(jnp.bfloat16)
    grad_flat = grad_conv.reshape(tok_count, chan_count).astype(jnp.float32)
    grad_key = masked(grad_flat * value_wide).astype(jnp.bfloat16)
    grad_value = masked(grad_flat * key_wide).astype(jnp.bfloat16)
    scale_factor = 1.0 / math.sqrt(lax.axis_size("dp") * tok_count * lax.axis_size("ctx"))
    taps_sum = lax.psum(
        taps_seq.reshape(tok_count, chan_count).astype(jnp.float32).astype(jnp.bfloat16), "dp"
    ).astype(jnp.float32)
    grad_taps = (taps_sum * scale_factor).astype(jnp.bfloat16)
    return (grad_gate[None], grad_key[None], grad_value[None], grad_taps)


def solution(mesh):
    return jax.shard_map(
        local,
        mesh=mesh,
        in_specs=(
            P("dp", "ctx", None),
            P("dp", "ctx", None),
            P("dp", "ctx", None),
            P("ctx", None),
            P("dp", "ctx", None),
            P("dp", "ctx"),
        ),
        out_specs=(
            P("dp", "ctx", None),
            P("dp", "ctx", None),
            P("dp", "ctx", None),
            P("ctx", None),
        ),
        check_vma=False,
    )
```

profile of v0, /device:TPU:1, one launch (start us, length us, event | category | flops | bytes accessed | tf_op | source)
XLA Modules:
  0.0 641.4 jit_solution(15273747222807358933)
XLA Ops:
  7.2 1.6 fusion.64
  9.8 17.0 %all-to-all-start.4 = ((bf16[1,4,64,512]{3,1,0,2:T(4,128)(2,1)}), bf16[1,4,64,512]{3,1,0,2:T(4,128)(2,1)S(1)}, u32[]{:S(2)}, u32[]{:S(2)}) async-start(bf16[1,4,64,512]{3,1,0,2:T(4,128)(2,1)} %copy.209), calls=%async_computation.4 | async-start | bytes 524288 | tf_op jit(solution)/shard_map/all_to_all | solution.py:44
  28.8 18.5 %all-to-all-done.4 = bf16[1,4,64,512]{3,1,0,2:T(4,128)(2,1)S(1)} async-done(((bf16[1,4,64,512]{3,1,0,2:T(4,128)(2,1)}), bf16[1,4,64,512]{3,1,0,2:T(4,128)(2,1)S(1)}, u32[]{:S(2)}, u32[]{:S(2)}) %all-to-all-start.4) | async-done | bytes 262176 | tf_op jit(solution)/shard_map/all_to_all | solution.py:44
  47.3 3.9 all-to-all-start
  53.6 2.1 copy.213
  55.7 26.1 %all-to-all-done = bf16[2,4,64,512]{3,1,0,2:T(4,128)(2,1)S(1)} async-done(((bf16[2,4,64,512]{3,1,0,2:T(4,128)(2,1)}), bf16[2,4,64,512]{3,1,0,2:T(4,128)(2,1)S(1)}, u32[]{:S(2)}, u32[]{:S(2)}) %all-to-all-start) | async-done | bytes 524320 | tf_op jit(solution)/shard_map/all_to_all | solution.py:44
  81.8 4.6 all-to-all-start.5
  89.6 4.1 copy.196
  93.7 44.4 %all-to-all-done.5 = bf16[2,1,256,2,512]{4,3,1,0,2:T(2,128)(2,1)S(1)} async-done(((bf16[2,1,256,2,512]{4,3,1,0,2:T(2,128)(2,1)}), bf16[2,1,256,2,512]{4,3,1,0,2:T(2,128)(2,1)S(1)}, u32[]{:S(2)}, u32[]{:S(2)}) %all-to-all-start.5) | async-done | bytes 1048608 | tf_op jit(solution)/shard_map/all_to_all | solution.py:49
  138.1 6.8 %all-to-all-start.1 = ((bf16[2,2,256,2,512]{4,3,1,0,2:T(2,128)(2,1)}), bf16[2,2,256,2,512]{4,3,1,0,2:T(2,128)(2,1)S(1)}, u32[]{:S(2)}, u32[]{:S(2)}) async-start(bf16[2,2,256,2,512]{4,3,1,0,2:T(2,128)(2,1)} %copy.196), calls=%async_computation.1 | async-start | bytes 4194304 | tf_op jit(solution)/shard_map/all_to_all | solution.py:49
  146.9 2.4 copy.216
  149.2 1.2 reshape.608
  150.9 1.4 fusion.18
  152.3 1.4 fusion.103
  153.7 86.9 %all-to-all-done.1 = bf16[2,2,256,2,512]{4,3,1,0,2:T(2,128)(2,1)S(1)} async-done(((bf16[2,2,256,2,512]{4,3,1,0,2:T(2,128)(2,1)}), bf16[2,2,256,2,512]{4,3,1,0,2:T(2,128)(2,1)S(1)}, u32[]{:S(2)}, u32[]{:S(2)}) %all-to-all-start.1) | async-done | bytes 2097184 | tf_op jit(solution)/shard_map/all_to_all | solution.py:49
  244.0 1.9 fusion.111
  247.1 2.1 copy.199
  249.2 1.5 squeeze.13
  250.7 2.1 fusion.9
  257.5 1.6 copy.200
  259.0 7.4 %all-to-all-start.2 = ((bf16[2,1,8,64,512]{4,2,1,0,3:T(8,128)(2,1)}), bf16[2,1,8,64,512]{4,2,1,0,3:T(8,128)(2,1)S(1)}, u32[]{:S(2)}, u32[]{:S(2)}) async-start(bf16[2,1,8,64,512]{4,2,1,0,3:T(8,128)(2,1)} %copy.200), calls=%async_computation.2 | async-start | bytes 2097152 | tf_op jit(solution)/shard_map/all_to_all | solution.py:81
  269.4 2.5 copy.217
  271.9 47.3 %all-to-all-done.2 = bf16[2,1,8,64,512]{4,2,1,0,3:T(8,128)(2,1)S(1)} async-done(((bf16[2,1,8,64,512]{4,2,1,0,3:T(8,128)(2,1)}), bf16[2,1,8,64,512]{4,2,1,0,3:T(8,128)(2,1)S(1)}, u32[]{:S(2)}, u32[]{:S(2)}) %all-to-all-start.2) | async-done | bytes 1048608 | tf_op jit(solution)/shard_map/all_to_all | solution.py:81
  319.2 5.9 all-to-all-start.6
  327.7 93.3 %all-to-all-done.6 = bf16[2,2,8,64,512]{4,2,1,0,3:T(8,128)(2,1)S(1)} async-done(((bf16[2,2,8,64,512]{4,2,1,0,3:T(8,128)(2,1)}), bf16[2,2,8,64,512]{4,2,1,0,3:T(8,128)(2,1)S(1)}, u32[]{:S(2)}, u32[]{:S(2)}) %all-to-all-start.6) | async-done | bytes 2097184 | tf_op jit(solution)/shard_map/all_to_all | solution.py:81
  421.0 7.3 %all-to-all-start.3 = ((bf16[1,128,2,512]{3,2,0,1:T(2,128)(2,1)}), bf16[1,128,2,512]{3,2,0,1:T(2,128)(2,1)S(1)}, u32[]{:S(2)}, u32[]{:S(2)}) async-start(bf16[1,128,2,512]{3,2,0,1:T(2,128)(2,1)} %copy.206), calls=%async_computation.3 | async-start | bytes 524288 | tf_op jit(solution)/shard_map/all_to_all | solution.py:86
  431.8 16.0 %all-to-all-done.3 = bf16[1,128,2,512]{3,2,0,1:T(2,128)(2,1)S(1)} async-done(((bf16[1,128,2,512]{3,2,0,1:T(2,128)(2,1)}), bf16[1,128,2,512]{3,2,0,1:T(2,128)(2,1)S(1)}, u32[]{:S(2)}, u32[]{:S(2)}) %all-to-all-start.3) | async-done | bytes 262176 | tf_op jit(solution)/shard_map/all_to_all | solution.py:86
  447.8 4.8 all-to-all-start.7
  455.3 26.7 %all-to-all-done.7 = bf16[2,128,2,512]{3,2,0,1:T(2,128)(2,1)S(1)} async-done(((bf16[2,128,2,512]{3,2,0,1:T(2,128)(2,1)}), bf16[2,128,2,512]{3,2,0,1:T(2,128)(2,1)S(1)}, u32[]{:S(2)}, u32[]{:S(2)}) %all-to-all-start.7) | async-done | bytes 524320 | tf_op jit(solution)/shard_map/all_to_all | solution.py:86
  484.0 2.6 fusion.58
  488.1 144.7 %all-reduce.2.cloned.1.call-done = bf16[256,512]{1,0:T(8,128)(2,1)} async-done(((bf16[256,512]{1,0:T(8,128)(2,1)}), bf16[256,512]{1,0:T(8,128)(2,1)}) %all-reduce.2.cloned.1.call-update) | async-done | bytes 262160 | tf_op jit(solution)/shard_map/psum | solution.py:147
  632.9 1.7 multiply_convert_fusion
  (92 shorter events, 35.0 us)
Async XLA Ops:
  7.2 19.6 %copy-start.6 = (bf16[1,256,512]{2,1,0:T(8,128)(2,1)S(1)}, bf16[1,256,512]{2,1,0:T(8,128)(2,1)}, u32[]{:S(2)}) copy-start(bf16[1,256,512]{2,1,0:T(8,128)(2,1)} %param.7) | copy-start | bytes 786436
  7.2 19.6 %copy-start.7 = (bf16[1,256,512]{2,1,0:T(8,128)(2,1)S(1)}, bf16[1,256,512]{2,1,0:T(8,128)(2,1)}, u32[]{:S(2)}) copy-start(bf16[1,256,512]{2,1,0:T(8,128)(2,1)} %param.8) | copy-start | bytes 786436
  8.8 18.6 %copy-start.10 = (s32[1,4]{1,0:T(1,128)S(1)}, s32[1,4]{1,0:T(1,128)}, u32[]{:S(2)}) copy-start(s32[1,4]{1,0:T(1,128)} %param.11) | copy-start | bytes 52
  8.9 18.6 %copy-start.9 = (bf16[256,512]{1,0:T(8,128)(2,1)S(1)}, bf16[256,512]{1,0:T(8,128)(2,1)}, u32[]{:S(2)}) copy-start(bf16[256,512]{1,0:T(8,128)(2,1)} %param.9) | copy-start | bytes 786436
  9.8 37.5 %all-to-all-start.4 = ((bf16[1,4,64,512]{3,1,0,2:T(4,128)(2,1)}), bf16[1,4,64,512]{3,1,0,2:T(4,128)(2,1)S(1)}, u32[]{:S(2)}, u32[]{:S(2)}) async-start(bf16[1,4,64,512]{3,1,0,2:T(4,128)(2,1)} %copy.209), calls=%async_computation.4 | async-start | bytes 524288 | tf_op jit(solution)/shard_map/all_to_all | solution.py:44
  47.3 34.5 %all-to-all-start = ((bf16[2,4,64,512]{3,1,0,2:T(4,128)(2,1)}), bf16[2,4,64,512]{3,1,0,2:T(4,128)(2,1)S(1)}, u32[]{:S(2)}, u32[]{:S(2)}) async-start(bf16[2,4,64,512]{3,1,0,2:T(4,128)(2,1)} %copy.191), calls=%async_computation | async-start | bytes 1048576 | tf_op jit(solution)/shard_map/all_to_all | solution.py:44
  81.8 56.3 %all-to-all-start.5 = ((bf16[2,1,256,2,512]{4,3,1,0,2:T(2,128)(2,1)}), bf16[2,1,256,2,512]{4,3,1,0,2:T(2,128)(2,1)S(1)}, u32[]{:S(2)}, u32[]{:S(2)}) async-start(bf16[2,1,256,2,512]{4,3,1,0,2:T(2,128)(2,1)} %copy.213), calls=%async_computation.5 | async-start | bytes 2097152 | tf_op jit(solution)/shard_map/all_to_all | solution.py:49
  138.1 102.5 %all-to-all-start.1 = ((bf16[2,2,256,2,512]{4,3,1,0,2:T(2,128)(2,1)}), bf16[2,2,256,2,512]{4,3,1,0,2:T(2,128)(2,1)S(1)}, u32[]{:S(2)}, u32[]{:S(2)}) async-start(bf16[2,2,256,2,512]{4,3,1,0,2:T(2,128)(2,1)} %copy.196), calls=%async_computation.1 | async-start | bytes 4194304 | tf_op jit(solution)/shard_map/all_to_all | solution.py:49
  150.5 1.8 copy-start.1
  245.9 1.2 copy-start
  252.8 1.0 copy-start.2
  252.8 1.4 copy-start.3
  252.8 1.7 copy-start.4
  259.0 60.2 %all-to-all-start.2 = ((bf16[2,1,8,64,512]{4,2,1,0,3:T(8,128)(2,1)}), bf16[2,1,8,64,512]{4,2,1,0,3:T(8,128)(2,1)S(1)}, u32[]{:S(2)}, u32[]{:S(2)}) async-start(bf16[2,1,8,64,512]{4,2,1,0,3:T(8,128)(2,1)} %copy.200), calls=%async_computation.2 | async-start | bytes 2097152 | tf_op jit(solution)/shard_map/all_to_all | solution.py:81
  319.2 101.8 %all-to-all-start.6 = ((bf16[2,2,8,64,512]{4,2,1,0,3:T(8,128)(2,1)}), bf16[2,2,8,64,512]{4,2,1,0,3:T(8,128)(2,1)S(1)}, u32[]{:S(2)}, u32[]{:S(2)}) async-start(bf16[2,2,8,64,512]{4,2,1,0,3:T(8,128)(2,1)} %copy.217), calls=%async_computation.6 | async-start | bytes 4194304 | tf_op jit(solution)/shard_map/all_to_all | solution.py:81
  421.0 26.8 %all-to-all-start.3 = ((bf16[1,128,2,512]{3,2,0,1:T(2,128)(2,1)}), bf16[1,128,2,512]{3,2,0,1:T(2,128)(2,1)S(1)}, u32[]{:S(2)}, u32[]{:S(2)}) async-start(bf16[1,128,2,512]{3,2,0,1:T(2,128)(2,1)} %copy.206), calls=%async_computation.3 | async-start | bytes 524288 | tf_op jit(solution)/shard_map/all_to_all | solution.py:86
  430.7 23.3 %copy-start.5 = (bf16[1,256,512]{2,1,0:T(8,128)(2,1)S(1)}, bf16[1,256,512]{2,1,0:T(8,128)(2,1)}, u32[]{:S(2)}) copy-start(bf16[1,256,512]{2,1,0:T(8,128)(2,1)} %param.10) | copy-start | bytes 786436
  447.8 34.2 %all-to-all-start.7 = ((bf16[2,128,2,512]{3,2,0,1:T(2,128)(2,1)}), bf16[2,128,2,512]{3,2,0,1:T(2,128)(2,1)S(1)}, u32[]{:S(2)}, u32[]{:S(2)}) async-start(bf16[2,128,2,512]{3,2,0,1:T(2,128)(2,1)} %copy.223), calls=%async_computation.7 | async-start | bytes 1048576 | tf_op jit(solution)/shard_map/all_to_all | solution.py:86
  452.6 180.2 %all-reduce.2.cloned.1.call-start = ((), (), s32[]{:S(2)}) async-start(), calls=%async_computation.8 | async-start | bytes 524288 | tf_op jit(solution)/shard_map/psum | solution.py:147
  482.3 1.7 copy-start.8
Sparse Core Ops, SparseCore 0:
  484.1 148.6 all-reduce.1
where the time goes:
time: 642 us; the launch traced here: 641 us
  waiting for transfers between devices  504 us (79%)
  starting transfers between devices  58 us (9%)
  local copies, waits for them, and re-layouts  35.6 us (6%)
  matrix products  20.7 us (3%)
  between operations  14.6 us (2%)
  other arithmetic  8.59 us (1%)
    psum x1, waiting for transfers between devices, local(): lax.psum(taps_seq.reshape(tok_count, chan_count).astype(jnp.float32).asty...  145 us
    all_to_all x2, waiting for transfers between devices, inverse_transform(): lax.all_to_all(twisted, 'ctx', split_axis=3, concat_axis=2, tiled=True)  141 us
    all_to_all x2, waiting for transfers between devices, forward_transform(): lax.all_to_all(packed, 'ctx', split_axis=2, concat_axis=3, tiled=True)  131 us
    all_to_all x2, waiting for transfers between devices, forward_transform(): lax.all_to_all(signals, 'ctx', split_axis=2, concat_axis=1, tiled=True)  44.6 us
    all_to_all x2, waiting for transfers between devices, inverse_transform(): lax.all_to_all(spread, 'ctx', split_axis=1, concat_axis=2, tiled=True)  42.7 us
    all_to_all x2, starting transfers between devices, forward_transform(): lax.all_to_all(signals, 'ctx', split_axis=2, concat_axis=1, tiled=True)  20.9 us
    all_to_all x2, starting transfers between devices, inverse_transform(): lax.all_to_all(twisted, 'ctx', split_axis=3, concat_axis=2, tiled=True)  13.3 us
  transfers between devices with their start and end apart: 9, of which 9 were waited for; matrix products, arithmetic and copies ran while one was open for 6% of the time, Pallas kernels for 0%

commit v1 on v0

--- a/solution.py
+++ b/solution.py
@@ -144,8 +144,11 @@
     grad_key = masked(grad_flat * value_wide).astype(jnp.bfloat16)
     grad_value = masked(grad_flat * key_wide).astype(jnp.bfloat16)
     scale_factor = 1.0 / math.sqrt(lax.axis_size("dp") * tok_count * lax.axis_size("ctx"))
-    taps_sum = lax.psum(
-        taps_seq.reshape(tok_count, chan_count).astype(jnp.float32).astype(jnp.bfloat16), "dp"
+    taps_sum = jnp.sum(
+        lax.all_gather(
+            taps_seq.reshape(tok_count, chan_count).astype(jnp.float32).astype(jnp.bfloat16), "dp"
+        ),
+        axis=0,
     ).astype(jnp.float32)
     grad_taps = (taps_sum * scale_factor).astype(jnp.bfloat16)
     return (grad_gate[None], grad_key[None], grad_value[None], grad_taps)

time: 642 us -> 514 us (0.80)
  waiting for transfers between devices: 504 us -> 196 us
  blocking collectives: 0 us -> 199 us
  starting transfers between devices: 58 us -> 38.4 us
    all_to_all x0 -> x3, blocking collectives: none -> 199 us  [the longest x2 162 us: inverse_transform(): lax.all_to_all(twisted, 'ctx', split_axis=3, concat_axis=2, tiled=True)]
    psum x1 -> x0, waiting for transfers between devices: 145 us -> none  [local(): lax.psum(taps_seq.reshape(tok_count, chan_count).astype(jnp.float32).asty...]
    all_to_all x2 -> x0, waiting for transfers between devices: 141 us -> none  [inverse_transform(): lax.all_to_all(twisted, 'ctx', split_axis=3, concat_axis=2, tiled=True)]
    all_to_all x2 -> x1, waiting for transfers between devices: 42.7 us -> 19.7 us  [inverse_transform(): lax.all_to_all(spread, 'ctx', split_axis=1, concat_axis=2, tiled=True)]
    all_to_all x2 -> x0, starting transfers between devices: 13.3 us -> none  [inverse_transform(): lax.all_to_all(twisted, 'ctx', split_axis=3, concat_axis=2, tiled=True)]
  transfers between devices with their start and end apart: 9 -> 6, of which waited for: 9 -> 5; matrix products, arithmetic and copies ran while one was open for 6% -> 7% of each run, Pallas kernels for 0% -> 0%
where the time goes in v1:
time: 514 us; the launch traced here: 511 us
  blocking collectives  199 us (39%)
  waiting for transfers between devices  196 us (38%)
  starting transfers between devices  38.4 us (7%)
  local copies, waits for them, and re-layouts  32.6 us (6%)
  matrix products  20.7 us (4%)
  between operations  14.6 us (3%)
  other arithmetic  10.5 us (2%)
    all_to_all x2, blocking collectives, inverse_transform(): lax.all_to_all(twisted, 'ctx', split_axis=3, concat_axis=2, tiled=True)  162 us
    all_to_all x2, waiting for transfers between devices, forward_transform(): lax.all_to_all(packed, 'ctx', split_axis=2, concat_axis=3, tiled=True)  131 us
    all_to_all x2, waiting for transfers between devices, forward_transform(): lax.all_to_all(signals, 'ctx', split_axis=2, concat_axis=1, tiled=True)  44.6 us
    all_to_all x1, blocking collectives, inverse_transform(): lax.all_to_all(spread, 'ctx', split_axis=1, concat_axis=2, tiled=True)  36.5 us
    all_to_all x2, starting transfers between devices, forward_transform(): lax.all_to_all(signals, 'ctx', split_axis=2, concat_axis=1, tiled=True)  20.9 us
    all_to_all x1, waiting for transfers between devices, inverse_transform(): lax.all_to_all(spread, 'ctx', split_axis=1, concat_axis=2, tiled=True)  19.7 us
    all_to_all x2, starting transfers between devices, forward_transform(): lax.all_to_all(packed, 'ctx', split_axis=2, concat_axis=3, tiled=True)  11.2 us
  transfers between devices with their start and end apart: 6, of which 5 were waited for; matrix products, arithmetic and copies ran while one was open for 7% of the time, Pallas kernels for 0%

profile of v1, /device:TPU:1, one launch (start us, length us, event | category | flops | bytes accessed | tf_op | source)
XLA Modules:
  0.0 511.1 jit_solution(9221389553091216282)
XLA Ops:
  7.2 1.6 fusion.64
  9.8 17.0 %all-to-all-start.4 = ((bf16[1,4,64,512]{3,1,0,2:T(4,128)(2,1)}), bf16[1,4,64,512]{3,1,0,2:T(4,128)(2,1)S(1)}, u32[]{:S(2)}, u32[]{:S(2)}) async-start(bf16[1,4,64,512]{3,1,0,2:T(4,128)(2,1)} %copy.209), calls=%async_computation.4 | async-start | bytes 524288 | tf_op jit(solution)/shard_map/all_to_all | solution.py:44
  27.6 1.2 copy.191
  28.8 18.5 %all-to-all-done.4 = bf16[1,4,64,512]{3,1,0,2:T(4,128)(2,1)S(1)} async-done(((bf16[1,4,64,512]{3,1,0,2:T(4,128)(2,1)}), bf16[1,4,64,512]{3,1,0,2:T(4,128)(2,1)S(1)}, u32[]{:S(2)}, u32[]{:S(2)}) %all-to-all-start.4) | async-done | bytes 262176 | tf_op jit(solution)/shard_map/all_to_all | solution.py:44
  47.3 3.9 all-to-all-start
  53.6 2.1 copy.213
  55.7 26.1 %all-to-all-done = bf16[2,4,64,512]{3,1,0,2:T(4,128)(2,1)S(1)} async-done(((bf16[2,4,64,512]{3,1,0,2:T(4,128)(2,1)}), bf16[2,4,64,512]{3,1,0,2:T(4,128)(2,1)S(1)}, u32[]{:S(2)}, u32[]{:S(2)}) %all-to-all-start) | async-done | bytes 524320 | tf_op jit(solution)/shard_map/all_to_all | solution.py:44
  81.8 4.6 all-to-all-start.5
  88.2 1.1 fusion.39
  89.6 4.1 copy.196
  93.7 44.4 %all-to-all-done.5 = bf16[2,1,256,2,512]{4,3,1,0,2:T(2,128)(2,1)S(1)} async-done(((bf16[2,1,256,2,512]{4,3,1,0,2:T(2,128)(2,1)}), bf16[2,1,256,2,512]{4,3,1,0,2:T(2,128)(2,1)S(1)}, u32[]{:S(2)}, u32[]{:S(2)}) %all-to-all-start.5) | async-done | bytes 1048608 | tf_op jit(solution)/shard_map/all_to_all | solution.py:49
  138.1 6.6 %all-to-all-start.1 = ((bf16[2,2,256,2,512]{4,3,1,0,2:T(2,128)(2,1)}), bf16[2,2,256,2,512]{4,3,1,0,2:T(2,128)(2,1)S(1)}, u32[]{:S(2)}, u32[]{:S(2)}) async-start(bf16[2,2,256,2,512]{4,3,1,0,2:T(2,128)(2,1)} %copy.196), calls=%async_computation.1 | async-start | bytes 4194304 | tf_op jit(solution)/shard_map/all_to_all | solution.py:49
  146.9 2.4 copy.216
  149.3 1.2 reshape.609
  150.9 1.4 fusion.18
  152.3 1.4 fusion.103
  153.7 86.8 %all-to-all-done.1 = bf16[2,2,256,2,512]{4,3,1,0,2:T(2,128)(2,1)S(1)} async-done(((bf16[2,2,256,2,512]{4,3,1,0,2:T(2,128)(2,1)}), bf16[2,2,256,2,512]{4,3,1,0,2:T(2,128)(2,1)S(1)}, u32[]{:S(2)}, u32[]{:S(2)}) %all-to-all-start.1) | async-done | bytes 2097184 | tf_op jit(solution)/shard_map/all_to_all | solution.py:49
  241.2 1.2 fusion.227
  242.5 1.1 copy.198
  244.0 1.9 fusion.111
  247.1 2.1 copy.199
  249.3 1.5 squeeze.13
  250.7 2.1 fusion.9
  254.6 1.1 fusion.33
  258.6 1.2 copy.217
  259.8 104.9 %all_to_all.117 = bf16[2,2,8,64,512]{4,2,1,0,3:T(8,128)(2,1)S(1)} all-to-all(bf16[2,2,8,64,512]{4,2,1,0,3:T(8,128)(2,1)S(1)} %copy.217), channel_id=1, replica_groups=mesh['dp'=16,'ctx'=32] {'ctx'}, dimensions={3} | all-to-all | bytes 4194304 | tf_op jit(solution)/shard_map/all_to_all | solution.py:81
  367.6 36.5 %all_to_all.118 = bf16[2,128,2,512]{3,2,0,1:T(2,128)(2,1)S(1)} all-to-all(bf16[2,128,2,512]{3,2,0,1:T(2,128)(2,1)S(1)} %copy.223), channel_id=1, replica_groups=mesh['dp'=16,'ctx'=32] {'ctx'}, dimensions={1} | all-to-all | bytes 1048576 | tf_op jit(solution)/shard_map/all_to_all | solution.py:86
  408.0 57.3 %all_to_all.119 = bf16[2,1,8,64,512]{4,2,1,0,3:T(8,128)(2,1)S(1)} all-to-all(bf16[2,1,8,64,512]{4,2,1,0,3:T(8,128)(2,1)S(1)} %copy.200), channel_id=1, replica_groups=mesh['dp'=16,'ctx'=32] {'ctx'}, dimensions={3} | all-to-all | bytes 2097152 | tf_op jit(solution)/shard_map/all_to_all | solution.py:81
  467.9 6.1 %all-to-all-start.3 = ((bf16[1,128,2,512]{3,2,0,1:T(2,128)(2,1)}), bf16[1,128,2,512]{3,2,0,1:T(2,128)(2,1)S(1)}, u32[]{:S(2)}, u32[]{:S(2)}) async-start(bf16[1,128,2,512]{3,2,0,1:T(2,128)(2,1)} %copy.206), calls=%async_computation.3 | async-start | bytes 524288 | tf_op jit(solution)/shard_map/all_to_all | solution.py:86
  474.2 19.7 %all-to-all-done.3 = bf16[1,128,2,512]{3,2,0,1:T(2,128)(2,1)S(1)} async-done(((bf16[1,128,2,512]{3,2,0,1:T(2,128)(2,1)}), bf16[1,128,2,512]{3,2,0,1:T(2,128)(2,1)S(1)}, u32[]{:S(2)}, u32[]{:S(2)}) %all-to-all-start.3) | async-done | bytes 262176 | tf_op jit(solution)/shard_map/all_to_all | solution.py:86
  496.6 2.6 fusion.58
  500.7 2.8 reduce_sum.12
  (90 shorter events, 29.8 us)
Async XLA Ops:
  7.2 19.6 %copy-start.6 = (bf16[1,256,512]{2,1,0:T(8,128)(2,1)S(1)}, bf16[1,256,512]{2,1,0:T(8,128)(2,1)}, u32[]{:S(2)}) copy-start(bf16[1,256,512]{2,1,0:T(8,128)(2,1)} %param.7) | copy-start | bytes 786436
  7.2 19.6 %copy-start.7 = (bf16[1,256,512]{2,1,0:T(8,128)(2,1)S(1)}, bf16[1,256,512]{2,1,0:T(8,128)(2,1)}, u32[]{:S(2)}) copy-start(bf16[1,256,512]{2,1,0:T(8,128)(2,1)} %param.8) | copy-start | bytes 786436
  8.8 18.6 %copy-start.10 = (s32[1,4]{1,0:T(1,128)S(1)}, s32[1,4]{1,0:T(1,128)}, u32[]{:S(2)}) copy-start(s32[1,4]{1,0:T(1,128)} %param.11) | copy-start | bytes 52
  8.9 18.6 %copy-start.9 = (bf16[256,512]{1,0:T(8,128)(2,1)S(1)}, bf16[256,512]{1,0:T(8,128)(2,1)}, u32[]{:S(2)}) copy-start(bf16[256,512]{1,0:T(8,128)(2,1)} %param.9) | copy-start | bytes 786436
  9.8 37.5 %all-to-all-start.4 = ((bf16[1,4,64,512]{3,1,0,2:T(4,128)(2,1)}), bf16[1,4,64,512]{3,1,0,2:T(4,128)(2,1)S(1)}, u32[]{:S(2)}, u32[]{:S(2)}) async-start(bf16[1,4,64,512]{3,1,0,2:T(4,128)(2,1)} %copy.209), calls=%async_computation.4 | async-start | bytes 524288 | tf_op jit(solution)/shard_map/all_to_all | solution.py:44
  47.3 34.5 %all-to-all-start = ((bf16[2,4,64,512]{3,1,0,2:T(4,128)(2,1)}), bf16[2,4,64,512]{3,1,0,2:T(4,128)(2,1)S(1)}, u32[]{:S(2)}, u32[]{:S(2)}) async-start(bf16[2,4,64,512]{3,1,0,2:T(4,128)(2,1)} %copy.191), calls=%async_computation | async-start | bytes 1048576 | tf_op jit(solution)/shard_map/all_to_all | solution.py:44
  81.8 56.3 %all-to-all-start.5 = ((bf16[2,1,256,2,512]{4,3,1,0,2:T(2,128)(2,1)}), bf16[2,1,256,2,512]{4,3,1,0,2:T(2,128)(2,1)S(1)}, u32[]{:S(2)}, u32[]{:S(2)}) async-start(bf16[2,1,256,2,512]{4,3,1,0,2:T(2,128)(2,1)} %copy.213), calls=%async_computation.5 | async-start | bytes 2097152 | tf_op jit(solution)/shard_map/all_to_all | solution.py:49
  138.1 102.5 %all-to-all-start.1 = ((bf16[2,2,256,2,512]{4,3,1,0,2:T(2,128)(2,1)}), bf16[2,2,256,2,512]{4,3,1,0,2:T(2,128)(2,1)S(1)}, u32[]{:S(2)}, u32[]{:S(2)}) async-start(bf16[2,2,256,2,512]{4,3,1,0,2:T(2,128)(2,1)} %copy.196), calls=%async_computation.1 | async-start | bytes 4194304 | tf_op jit(solution)/shard_map/all_to_all | solution.py:49
  144.7 356.0 %all-gather.2.cloned.1.call-start = ((), (), s32[]{:S(2)}) async-start(), calls=%async_computation.8 | async-start | bytes 4456448 | tf_op jit(solution)/shard_map/all_gather | solution.py:148
  150.5 1.8 copy-start.1
  245.9 1.2 copy-start
  252.9 1.0 copy-start.2
  252.9 1.4 copy-start.3
  252.9 1.7 copy-start.4
  466.2 28.5 %copy-start.5 = (bf16[1,256,512]{2,1,0:T(8,128)(2,1)S(1)}, bf16[1,256,512]{2,1,0:T(8,128)(2,1)}, u32[]{:S(2)}) copy-start(bf16[1,256,512]{2,1,0:T(8,128)(2,1)} %param.10) | copy-start | bytes 786436
  467.9 25.9 %all-to-all-start.3 = ((bf16[1,128,2,512]{3,2,0,1:T(2,128)(2,1)}), bf16[1,128,2,512]{3,2,0,1:T(2,128)(2,1)S(1)}, u32[]{:S(2)}, u32[]{:S(2)}) async-start(bf16[1,128,2,512]{3,2,0,1:T(2,128)(2,1)} %copy.206), calls=%async_computation.3 | async-start | bytes 524288 | tf_op jit(solution)/shard_map/all_to_all | solution.py:86
  494.1 2.4 copy-start.8
Sparse Core Ops, SparseCore 0:
  405.7 69.6 all-gather.1
